TPU v7x, 256 devices: a whole 4x4x8 slice. The times are simulated.
256 devices in a mesh: tok: 8 (over y, x_hi), fin: 8 (over z), fout: 4 (over x_lo, core).
Axes of the slice: x: 4 (x_hi: 2, x_lo: 2; x = x_hi * 2 + x_lo), y: 4, z: 8, core: 2. Of those that a mesh axis runs over, the one named last changes fastest.
Arguments:
- tokens_in: bfloat16 [512, 8192], P(('tok', 'fout'), 'fin'), may hold values from -2 to 2
- cotangent: bfloat16 [512, 8192], P(('tok', 'fout'), 'fin'), may hold values from -0.19921875 to 0.19921875
- gate_weight: bfloat16 [8192, 28672], P('fin', ('tok', 'fout')), may hold values from -0.21875 to 0.21875
- up_weight: bfloat16 [8192, 28672], P('fin', ('tok', 'fout')), may hold values from -0.21875 to 0.21875
- down_weight: bfloat16 [28672, 8192], P(('tok', 'fout'), 'fin'), may hold values from -0.75 to 0.75
Outputs:
- input_grad: bfloat16 [512, 8192], P(('tok', 'fout'), 'fin')
- gate_weight_grad: bfloat16 [8192, 28672], P('fin', ('tok', 'fout'))
- up_weight_grad: bfloat16 [8192, 28672], P('fin', ('tok', 'fout'))
- down_weight_grad: bfloat16 [28672, 8192], P(('tok', 'fout'), 'fin')
All inputs are finite; a program needn't handle non-finite values.
Results may differ from a plain program's by a relative error of at most 0.033.
Values may be sent and summed in bfloat16 or wider, within the bound.
A program may use at most 64 MiB of HBM per device.

v0:
```python
import jax
import jax.numpy as jnp
from jax import lax
from jax.sharding import PartitionSpec as P


def contract_last(first_op, second_op):
    return lax.dot_general(
        first_op, second_op, (((1,), (1,)), ((), ())), preferred_element_type=jnp.float32
    )


def contract_first(first_op, second_op):
    return lax.dot_general(
        first_op, second_op, (((0,), (0,)), ((), ())), preferred_element_type=jnp.float32
    )


def activations(gate_sum, up_sum, hidden_grad):
    sigmoid_gate = jax.nn.sigmoid(gate_sum)
    silu_gate = gate_sum * sigmoid_gate
    hidden = (silu_gate * up_sum).astype(jnp.bfloat16)
    gate_grad = (
        hidden_grad * up_sum * sigmoid_gate * (1.0 + gate_sum * (1.0 - sigmoid_gate))
    ).astype(jnp.bfloat16)
    up_grad = (hidden_grad * silu_gate).astype(jnp.bfloat16)
    return (hidden, gate_grad, up_grad)


def local(tokens_in, cotangent, gate_weight, up_weight, down_weight):
    inputs, grads_out = (
        lax.all_gather(tokens_in, ("tok", "fout"), axis=0, tiled=True),
        lax.all_gather(cotangent, ("tok", "fout"), axis=0, tiled=True),
    )
    gate_part = jnp.dot(inputs, gate_weight, preferred_element_type=jnp.float32)
    up_part = jnp.dot(inputs, up_weight, preferred_element_type=jnp.float32)
    gate_sum, up_sum = (
        lax.psum(gate_part.astype(jnp.bfloat16), "fin").astype(jnp.float32),
        lax.psum(up_part.astype(jnp.bfloat16), "fin").astype(jnp.float32),
    )
    hidden_grad = lax.psum(
        contract_last(grads_out, down_weight).astype(jnp.bfloat16), "fin"
    ).astype(jnp.float32)
    hidden, gate_grad, up_grad = activations(gate_sum, up_sum, hidden_grad)
    down_weight_grad = contract_first(hidden, grads_out).astype(jnp.bfloat16)
    gate_weight_grad = contract_first(inputs, gate_grad).astype(jnp.bfloat16)
    up_weight_grad = contract_first(inputs, up_grad).astype(jnp.bfloat16)
    input_grad = lax.psum_scatter(
        (contract_last(gate_grad, gate_weight) + contract_last(up_grad, up_weight)).astype(
            jnp.bfloat16
        ),
        ("tok", "fout"),
        scatter_dimension=0,
        tiled=True,
    )
    return (input_grad, gate_weight_grad, up_weight_grad, down_weight_grad)


def solution(mesh):
    in_specs = (
        P(("tok", "fout"), "fin"),
        P(("tok", "fout"), "fin"),
        P("fin", ("tok", "fout")),
        P("fin", ("tok", "fout")),
        P(("tok", "fout"), "fin"),
    )
    out_specs = (
        P(("tok", "fout"), "fin"),
        P("fin", ("tok", "fout")),
        P("fin", ("tok", "fout")),
        P(("tok", "fout"), "fin"),
    )
    return jax.shard_map(local, mesh=mesh, in_specs=in_specs, out_specs=out_specs, check_vma=False)
```

profile of v0, /device:TPU:4, one launch (start us, length us, event | category | flops | bytes accessed | tf_op | source)
XLA Modules:
  0.0 300.2 jit_solution(11693189449983142367)
XLA Ops:
  7.2 0.0 copy-start
  7.2 0.0 all-gather.5.cloned.1.call-start
  7.2 0.7 all-gather.5.cloned.1.call-update
  7.9 0.0 all-gather.3.cloned.1.call-start
  8.0 0.7 all-gather.3.cloned.1.call-update
  8.7 0.0 all-reduce.3.cloned.1.call-start
  8.7 52.2 %all-gather.5.cloned.1.call-done = bf16[512,1024]{1,0:T(8,128)(2,1)} async-done(((bf16[16,1024]{1,0:T(8,128)(2,1)}), bf16[512,1024]{1,0:T(8,128)(2,1)}) %all-gather.5.cloned.1.call-update) | async-done | bytes 1048592 | tf_op jit(solution)/shard_map/all_gather | solution.py:32
  60.9 0.0 copy-start.6
  60.9 4.1 %convolution_convert_fusion.2 = bf16[512,896]{1,0:T(8,128)(2,1)} fusion(bf16[512,1024]{1,0:T(8,128)(2,1)} %all-gather.5.cloned.1.call-done, bf16[1024,896]{1,0:T(8,128)(2,1)} %param.8), kind=kOutput, calls=%fused_computation.20 | convolution fusion | flops 939982848 | bytes 3801088 | tf_op jit(solution)/shard_map/dot_general | solution.py:36
  65.0 0.0 copy-done
  65.0 0.0 copy-done.6
  65.0 2.2 convolution_convert_fusion.1
  67.2 43.5 %all-gather.3.cloned.1.call-done = bf16[512,1024]{1,0:T(8,128)(2,1)} async-done(((bf16[16,1024]{1,0:T(8,128)(2,1)}), bf16[512,1024]{1,0:T(8,128)(2,1)}) %all-gather.3.cloned.1.call-update) | async-done | bytes 1048592 | tf_op jit(solution)/shard_map/all_gather | solution.py:33
  110.7 4.0 %convolution_convert_fusion.3 = bf16[512,896]{1,0:T(8,128)(2,1)} fusion(bf16[512,1024]{1,0:T(8,128)(2,1)} %all-gather.3.cloned.1.call-done, bf16[896,1024]{1,0:T(8,128)(2,1)} %param.9), kind=kOutput, calls=%fused_computation.21 | convolution fusion | flops 939982848 | bytes 3801088 | tf_op jit(solution)/shard_map/dot_general | solution.py:8
  114.7 0.0 all-reduce.3.cloned.1.call-update
  114.7 0.0 reduce-scatter.2.cloned.1.call-start
  114.8 87.5 %all-reduce.3.cloned.1.call-done = (bf16[512,896]{1,0:T(8,128)(2,1)}, bf16[512,896]{1,0:T(8,128)(2,1)}, bf16[512,896]{1,0:T(8,128)(2,1)}) async-done(((bf16[512,896]{1,0:T(8,128)(2,1)}, bf16[512,896]{1,0:T(8,128)(2,1)}, bf16[512,896]{1,0:T(8,128)(2,1)}), (bf16[512,896]{1,0:T(8,128)(2,1)}, bf16[512,896]{1,0:T(8,128)(2,1)}, bf16[512,896]{1,0:T(8,128)(2,1)})) %all-reduce.3.cloned.1.call-update) | async-done | bytes 2752528 | tf_op jit(solution)/shard_map/psum | solution.py:39
  202.2 2.6 fusion.3
  204.8 0.0 copy-start.4
  204.8 0.9 copy-done.4
  205.7 0.0 copy-start.2
  205.7 0.0 copy-start.3
  205.7 0.0 copy-start.5
  205.7 1.3 fusion.13
  207.0 0.0 copy-done.2
  207.0 0.2 copy-done.3
  207.2 0.6 copy-done.5
  207.8 2.3 add_convert_fusion
  210.1 0.0 reduce-scatter.2.cloned.1.call-update
  210.2 3.9 %convert_bitcast_fusion.1 = bf16[1024,896]{0,1:T(8,128)(2,1)} fusion(bf16[512,896]{1,0:T(8,128)(2,1)} %copy-done.4, bf16[512,1024]{1,0:T(8,128)(2,1)} %all-gather.5.cloned.1.call-done), kind=kOutput, calls=%fused_computation.17 | convolution fusion | flops 940441600 | bytes 3801088 | tf_op jit(solution)/shard_map/dot_general | solution.py:14
  214.0 3.8 %copy.9 = bf16[1024,896]{1,0:T(8,128)(2,1)} copy(bf16[1024,896]{0,1:T(8,128)(2,1)} %convert_bitcast_fusion.1) | data formatting | bytes 3670016
  217.8 4.0 %convert_bitcast_fusion = bf16[1024,896]{0,1:T(8,128)(2,1)} fusion(bf16[512,1024]{1,0:T(8,128)(2,1)} %all-gather.5.cloned.1.call-done, bf16[512,896]{1,0:T(8,128)(2,1)} %get-tuple-element.9, bf16[512,896]{1,0:T(8,128)(2,1)S(1)} %copy-done.2), kind=kOutput, calls=%fused_computation.16 | convolution fusion | flops 944111616 | bytes 4718592 | tf_op jit(solution)/shard_map/dot_general | solution.py:14
  221.8 0.0 copy-start.1
  221.8 3.9 %copy.10 = bf16[1024,896]{1,0:T(8,128)(2,1)} copy(bf16[1024,896]{0,1:T(8,128)(2,1)} %convert_bitcast_fusion) | data formatting | bytes 3670016
  225.7 0.0 copy-done.1
  225.7 4.0 %convolution_convert_fusion = bf16[896,1024]{1,0:T(8,128)(2,1)} fusion(bf16[512,1024]{1,0:T(8,128)(2,1)} %all-gather.3.cloned.1.call-done, bf16[512,896]{1,0:T(8,128)(2,1)S(1)} %copy-done.1, bf16[512,896]{1,0:T(8,128)(2,1)} %get-tuple-element.10), kind=kOutput, calls=%fused_computation.18 | convolution fusion | flops 944111616 | bytes 4718592 | tf_op jit(solution)/shard_map/dot_general | solution.py:14
  229.8 63.9 %reduce-scatter.2.cloned.1.call-done = bf16[16,1024]{1,0:T(8,128)(2,1)} async-done(((bf16[512,1024]{1,0:T(8,128)(2,1)}), bf16[16,1024]{1,0:T(8,128)(2,1)}) %reduce-scatter.2.cloned.1.call-update) | async-done | bytes 32784 | tf_op jit(solution)/shard_map/reduce_scatter | solution.py:48
Async XLA Ops:
  7.2 57.8 %copy-start = (bf16[1024,896]{1,0:T(8,128)(2,1)S(1)}, bf16[1024,896]{1,0:T(8,128)(2,1)}, u32[]{:S(2)}) copy-start(bf16[1024,896]{1,0:T(8,128)(2,1)} %param.7) | copy-start | bytes 5505028
  7.2 53.7 %all-gather.5.cloned.1.call-start = ((), (), s32[]{:S(2)}) async-start(), calls=%async_computation.2 | async-start | bytes 1081344 | tf_op jit(solution)/shard_map/all_gather | solution.py:32
  7.9 102.7 %all-gather.3.cloned.1.call-start = ((), (), s32[]{:S(2)}) async-start(), calls=%async_computation.1 | async-start | bytes 1081344 | tf_op jit(solution)/shard_map/all_gather | solution.py:33
  8.7 193.6 %all-reduce.3.cloned.1.call-start = ((), (), s32[]{:S(2)}) async-start(), calls=%async_computation.4 | async-start | bytes 5505024 | tf_op jit(solution)/shard_map/psum | solution.py:39
  60.9 4.1 %copy-start.6 = (bf16[512,1024]{1,0:T(8,128)(2,1)S(1)}, bf16[512,1024]{1,0:T(8,128)(2,1)}, u32[]{:S(2)}) copy-start(bf16[512,1024]{1,0:T(8,128)(2,1)} %all-gather.5.cloned.1.call-done) | copy-start | bytes 3145732
  114.7 179.0 %reduce-scatter.2.cloned.1.call-start = ((), (), s32[]{:S(2)}) async-start(), calls=%async_computation.3 | async-start | bytes 1081344 | tf_op jit(solution)/shard_map/reduce_scatter | solution.py:48
  204.8 0.9 copy-start.4
  205.7 1.3 copy-start.2
  205.7 1.5 copy-start.3
  205.7 2.1 copy-start.5
  221.8 3.9 %copy-start.1 = (bf16[512,896]{1,0:T(8,128)(2,1)S(1)}, bf16[512,896]{1,0:T(8,128)(2,1)}, u32[]{:S(2)}) copy-start(bf16[512,896]{1,0:T(8,128)(2,1)} %get-tuple-element.8) | copy-start | bytes 2752516
Sparse Core Ops, SparseCore 0:
  10.6 50.2 all-gather.4
  63.5 47.1 all-gather.2
  114.8 87.3 all-reduce.2
  210.3 83.3 reduce-scatter.1
where the time goes:
time: 301 us; the launch traced here: 300 us
  waiting for transfers between devices  248 us (82%)
  matrix products  25.8 us (9%)
  between operations  13.8 us (5%)
  local copies, waits for them, and re-layouts  9.4 us (3%)
    psum x1, waiting for transfers between devices, local(): lax.psum(up_part.astype(jnp.bfloat16), 'fin').astype(jnp.float32)  87.5 us
    reduce_scatter x1, waiting for transfers between devices, local(): lax.psum_scatter((contract_last(gate_grad, gate_weight) + contract_last(u...  63.9 us
    all_gather x1, waiting for transfers between devices, local(): lax.all_gather(tokens_in, ('tok', 'fout'), axis=0, tiled=True)  52.2 us
    all_gather x1, waiting for transfers between devices, local(): lax.all_gather(cotangent, ('tok', 'fout'), axis=0, tiled=True)  43.5 us
    dot_general x3, matrix products, contract_first(): lax.dot_general(first_op, second_op, (((0,), (0,)), ((), ())), preferred_...  11.9 us
    unnamed x16, local copies, waits for them, and re-layouts  9.4 us
    dot_general x3, matrix products, contract_last(): lax.dot_general(first_op, second_op, (((1,), (1,)), ((), ())), preferred_...  7.66 us
  transfers between devices with their start and end apart: 4, of which 4 were waited for; matrix products, arithmetic and copies ran while one was open for 9% of the time, Pallas kernels for 0%

commit v1 on v0

v1 whole, which is shorter than its diff:
```python
import functools

import jax
import jax.numpy as jnp
from jax import lax
from jax.experimental import pallas as pl
from jax.experimental.pallas import tpu as pltpu
from jax.sharding import PartitionSpec as P

MESH = pl.DeviceIdType.MESH
BF = jnp.bfloat16
F32 = jnp.float32
NT = (((1,), (1,)), ((), ()))
DY = (0, 1, 3, 2)
DX = (1, 3, 2)
NZ = 8
NR = 4


def kernel(
    x_hbm, ct_hbm, wg_hbm, wu_hbm, wd_hbm,
    ig_out, dwg_out, dwu_out, dwd_out,
    xb, xt, wg, wu, wd, pt, sdn, sup, rdn, rup, gb, acc, igs, igr, iys, iyr, igacc,
    w_sem, xs_sem, xr_sem, ys_sem, yr_sem, cs_sem, cr_sem,
    rs_s, rs_r, ag_s, ag_r, is_s, is_r, iy_s, iy_r,
):
    tok, z, fout = lax.axis_index("tok"), lax.axis_index("fin"), lax.axis_index("fout")
    y, x = tok // 2, (tok % 2) * 2 + fout // 2
    core = fout % 2
    me = x * 2 + core

    def at(y_, x_, c_, z_):
        return dict(tok=y_ * 2 + x_ // 2, fin=z_, fout=(x_ % 2) * 2 + c_)

    def row_peer(k):
        j = (me + k) % 8
        return at(y, j // 2, j % 2, z)

    partner = at(y, x, 1 - core, z)
    xpeer = [at(y, (x + d) % 4, core, z) for d in DX]
    ypeer = [None] + [at((y + d) % 4, x, core, z) for d in DY[1:]]
    zdn = at(y, x, core, (z + NZ - 1) % NZ)
    zup = at(y, x, core, (z + 1) % NZ)

    def rcopy(src, dst, ss, rs, dev):
        return pltpu.make_async_remote_copy(
            src_ref=src, dst_ref=dst, send_sem=ss, recv_sem=rs, device_id=dev, device_id_type=MESH
        )

    sends = []

    def start(copy):
        copy.start()
        sends.append(copy)

    loads = [
        pltpu.make_async_copy(x_hbm, xb.at[0, me, 0], w_sem.at[0]),
        pltpu.make_async_copy(ct_hbm, xb.at[0, me, 1], w_sem.at[1]),
        pltpu.make_async_copy(wg_hbm, wg, w_sem.at[2]),
        pltpu.make_async_copy(wu_hbm, wu, w_sem.at[3]),
        pltpu.make_async_copy(wd_hbm, wd, w_sem.at[4]),
    ]
    for c in loads:
        c.start()

    bar = pltpu.get_barrier_semaphore()
    everyone = [row_peer(k) for k in range(1, 8)] + ypeer[1:] + [zdn, zup]
    for p in everyone:
        pl.semaphore_signal(bar, inc=1, device_id=p, device_id_type=MESH)
    pl.semaphore_wait(bar, len(everyone))

    loads[0].wait()
    loads[1].wait()

    def x_copy(i):
        return rcopy(xb.at[0, me], xb.at[0, me], xs_sem.at[i], xr_sem.at[i], xpeer[i])

    def blk(k):
        return me if k == 0 else ((x + DX[k - 1]) % 4) * 2 + core

    REV = {1: 3, 3: 1, 2: 2}

    def y_copy(r, k):
        rr = DY.index((4 - DY[r]) % 4)
        return rcopy(xb.at[0, blk(k)], xb.at[rr, blk(k)], ys_sem.at[r, k], yr_sem.at[rr, k], ypeer[r])

    def c_copy(r, k):
        return rcopy(xb.at[r, blk(k)], xb.at[r, blk(k)], cs_sem.at[r, k], cr_sem.at[r, k], partner)

    def x_recv(i):
        n = DX.index(REV[DX[i]])
        return rcopy(xb.at[0, blk(i + 1)], xb.at[0, blk(i + 1)], xs_sem.at[n], xr_sem.at[n], xpeer[i])

    def y_recv(r, k):
        return rcopy(xb.at[r, blk(k)], xb.at[r, blk(k)], ys_sem.at[r, k], yr_sem.at[r, k], ypeer[r])

    def c_recv(r, k):
        b = blk(k) + 1 - 2 * core
        return rcopy(xb.at[r, b], xb.at[r, b], cs_sem.at[r, k], cr_sem.at[r, k], partner)

    for i in range(3):
        start(x_copy(i))
    start(c_copy(0, 0))
    for r in (1, 2):
        start(y_copy(r, 0))
    for i in range(3):
        x_recv(i).wait_recv()
        start(c_copy(0, i + 1))
        for r in (1, 2):
            start(y_copy(r, i + 1))
    for k in range(4):
        start(y_copy(3, k))

    def gather_done(r):
        if r > 0:
            for k in range(4):
                y_recv(r, k).wait_recv()
                start(c_copy(r, k))
        for k in range(4):
            c_recv(r, k).wait_recv()

    nd = [4, 3, 4, 3]

    def partials(r):
        gather_done(r)
        if r == 0:
            for c in loads[2:]:
                c.wait()
        toks = xb[r, :, 0].reshape(128, 1024)
        cots = xb[r, :, 1].reshape(128, 1024)
        pt[r, :, 0] = jnp.dot(toks, wg[...], preferred_element_type=F32).reshape(8, 16, 896)
        pt[r, :, 1] = jnp.dot(toks, wu[...], preferred_element_type=F32).reshape(8, 16, 896)
        pt[r, :, 2] = lax.dot_general(cots, wd[...], NT, preferred_element_type=F32).reshape(8, 16, 896)
        send_sums(r, 0)
        xt[r] = toks.T

    def dn_copy(r, s):
        return rcopy(sdn.at[r, s], rdn.at[r, s], rs_s.at[r, 0, s], rs_r.at[r, 0, s], zdn)

    def up_copy(r, s):
        return rcopy(sup.at[r, s], rup.at[r, s], rs_s.at[r, 1, s], rs_r.at[r, 1, s], zup)

    def send_sums(r, s):
        n, m = nd[r], 7 - nd[r]
        if s < n:
            mine = pt[r, (z - n + s + NZ) % NZ]
            if s > 0:
                dn_copy(r, s - 1).wait_recv()
                mine = mine + rdn[r, s - 1].astype(F32)
            sdn[r, s] = mine.astype(BF)
            start(dn_copy(r, s))
        if s < m:
            mine = pt[r, (z + m - s) % NZ]
            if s > 0:
                up_copy(r, s - 1).wait_recv()
                mine = mine + rup[r, s - 1].astype(F32)
            sup[r, s] = mine.astype(BF)
            start(up_copy(r, s))

    def ag_copy(r, d, t):
        c = (z + t) % NZ if d == 0 else (z - t + NZ) % NZ
        return rcopy(gb.at[r, c], gb.at[r, c], ag_s.at[r, d, t], ag_r.at[r, d, t], zdn if d == 0 else zup)

    def ag_recv(r, d, t):
        c = (z + t + 1) % NZ if d == 0 else (z - t - 1 + NZ) % NZ
        return rcopy(gb.at[r, c], gb.at[r, c], ag_s.at[r, d, t], ag_r.at[r, d, t], zdn if d == 0 else zup)

    def act(r):
        n, m = nd[r], 7 - nd[r]
        dn_copy(r, n - 1).wait_recv()
        up_copy(r, m - 1).wait_recv()
        total = pt[r, z] + rdn[r, n - 1].astype(F32) + rup[r, m - 1].astype(F32)
        g, u, hg = total[0], total[1], total[2]
        s = jax.nn.sigmoid(g)
        silu = g * s
        gb[r, z, 0] = (silu * u).astype(BF)
        gb[r, z, 1] = (hg * u * s * (1.0 + g * (1.0 - s))).astype(BF)
        gb[r, z, 2] = (hg * silu).astype(BF)

    def spread(r, t):
        hops = (7 - nd[r], nd[r])
        for d in (0, 1):
            if t > 0 and t <= hops[d]:
                ag_recv(r, d, t - 1).wait_recv()
            if t < hops[d]:
                start(ag_copy(r, d, t))

    def stage(r, s):
        if s < 4:
            send_sums(r, s)
        elif s == 4:
            act(r)
            spread(r, 0)
        else:
            spread(r, s - 4)

    def ig_copy(r, k):
        j = (me + k) % 8
        return rcopy(igs.at[r, j], igr.at[r, 8 - k], is_s.at[r, k], is_r.at[r, 8 - k], row_peer(k))

    def ig_recv(r, k):
        return rcopy(igs.at[r, 0], igr.at[r, k], is_s.at[r, k], is_r.at[r, k], row_peer(k))

    def input_part(r):
        gg = gb[r, :, 1].reshape(128, 896)
        ug = gb[r, :, 2].reshape(128, 896)
        part = lax.dot_general(gg, wg[...], NT, preferred_element_type=F32)
        part = part + lax.dot_general(ug, wu[...], NT, preferred_element_type=F32)
        igs[r] = part.astype(BF).reshape(8, 16, 1024)
        for k in range(1, 8):
            start(ig_copy(r, k))

    def add_dw(r, i, lhs_t, rhs, out, rows):
        step = 128
        def body(m, _):
            sl = pl.ds(pl.multiple_of(m * step, step), step)
            v = jnp.dot(lhs_t[sl, :], rhs, preferred_element_type=F32)
            if r > 0:
                v = v + acc[i, sl, :rhs.shape[1]]
            if r < NR - 1:
                acc[i, sl, :rhs.shape[1]] = v
            else:
                out[sl, :] = v.astype(BF)
            return 0
        lax.fori_loop(0, rows // step, body, 0)

    def dw_gate(r):
        add_dw(r, 0, xt.at[r], gb[r, :, 1].reshape(128, 896), dwg_out, 1024)

    def dw_up(r):
        add_dw(r, 1, xt.at[r], gb[r, :, 2].reshape(128, 896), dwu_out, 1024)

    def dw_down(r):
        xt[r, :896] = gb[r, :, 0].reshape(128, 896).T
        add_dw(r, 2, xt.at[r], xb[r, :, 1].reshape(128, 1024), dwd_out, 896)

    def iy_copy(r):
        return rcopy(iys.at[r], iyr.at[r], iy_s.at[r], iy_r.at[r], ypeer[r])

    def row_sum(r):
        for k in range(1, 8):
            ig_recv(r, k).wait_recv()
        v = igs[r, me].astype(F32)
        for k in range(1, 8):
            v = v + igr[r, k].astype(F32)
        if r == 0:
            igacc[...] = v
        else:
            iys[r] = v.astype(BF)
            start(iy_copy(r))

    partials(0)
    stage(0, 1)
    partials(1)
    partials(2)
    stage(0, 2)
    stage(1, 1)
    stage(2, 1)
    partials(3)
    done = [2, 1, 1, 0]
    while min(done) < 8:
        for r in range(4):
            if done[r] < 8:
                done[r] += 1
                stage(r, done[r])
                if done[r] == 8:
                    input_part(r)
                    dw_gate(r)
                    dw_up(r)
                    if r > 0:
                        row_sum(r - 1)
                    dw_down(r)
    row_sum(3)
    total = igacc[...]
    for r in range(1, 4):
        iy_copy(r).wait_recv()
        total = total + iyr[r].astype(F32)
    ig_out[...] = total.astype(BF)
    for c in sends:
        c.wait_send()


def local(tokens_in, cotangent, gate_weight, up_weight, down_weight):
    vm = pltpu.VMEM
    dma = pltpu.SemaphoreType.DMA
    return pl.pallas_call(
        kernel,
        out_shape=(
            jax.ShapeDtypeStruct((16, 1024), BF),
            jax.ShapeDtypeStruct((1024, 896), BF),
            jax.ShapeDtypeStruct((1024, 896), BF),
            jax.ShapeDtypeStruct((896, 1024), BF),
        ),
        in_specs=[pl.BlockSpec(memory_space=pl.ANY)] * 5,
        out_specs=[pl.BlockSpec(memory_space=pltpu.VMEM)] * 4,
        scratch_shapes=[
            vm((4, 8, 2, 16, 1024), BF),
            vm((4, 1024, 128), BF),
            vm((1024, 896), BF),
            vm((1024, 896), BF),
            vm((896, 1024), BF),
            vm((4, 8, 3, 16, 896), F32),
            vm((4, 4, 3, 16, 896), BF),
            vm((4, 4, 3, 16, 896), BF),
            vm((4, 4, 3, 16, 896), BF),
            vm((4, 4, 3, 16, 896), BF),
            vm((4, 8, 3, 16, 896), BF),
            vm((3, 1024, 1024), F32),
            vm((4, 8, 16, 1024), BF),
            vm((4, 8, 16, 1024), BF),
            vm((4, 16, 1024), BF),
            vm((4, 16, 1024), BF),
            vm((16, 1024), F32),
            dma((5,)),
            dma((3,)), dma((3,)),
            dma((4, 4)), dma((4, 4)),
            dma((4, 4)), dma((4, 4)),
            dma((4, 2, 4)), dma((4, 2, 4)),
            dma((4, 2, 4)), dma((4, 2, 4)),
            dma((4, 8)), dma((4, 8)),
            dma((4,)), dma((4,)),
        ],
        compiler_params=pltpu.CompilerParams(
            collective_id=0, has_side_effects=True, vmem_limit_bytes=56 * 2**20
        ),
        cost_estimate=pl.CostEstimate(flops=7_516_000_000, bytes_accessed=11_000_000, transcendentals=0),
    )(tokens_in, cotangent, gate_weight, up_weight, down_weight)


def solution(mesh):
    in_specs = (
        P(("tok", "fout"), "fin"),
        P(("tok", "fout"), "fin"),
        P("fin", ("tok", "fout")),
        P("fin", ("tok", "fout")),
        P(("tok", "fout"), "fin"),
    )
    out_specs = (
        P(("tok", "fout"), "fin"),
        P("fin", ("tok", "fout")),
        P("fin", ("tok", "fout")),
        P(("tok", "fout"), "fin"),
    )
    return jax.shard_map(local, mesh=mesh, in_specs=in_specs, out_specs=out_specs, check_vma=False)
```

time: 301 us -> 116 us (0.39)
  waiting for transfers between devices: 248 us -> 0 us
  Pallas kernels: 0 us -> 106 us
  matrix products: 25.8 us -> 0 us
  between operations: 13.8 us -> 0.64 us
    pallas_call x0 -> x1, Pallas kernels: none -> 106 us  [local(): pl.pallas_call(kernel, out_shape=(jax.ShapeDtypeStruct((16, 1024), BF), j...]
    all_gather x2 -> x0, waiting for transfers between devices: 95.7 us -> none  [the longest x1 52.2 us: local(): lax.all_gather(tokens_in, ('tok', 'fout'), axis=0, tiled=True)]
    psum x1 -> x0, waiting for transfers between devices: 87.5 us -> none  [local(): lax.psum(up_part.astype(jnp.bfloat16), 'fin').astype(jnp.float32)]
    reduce_scatter x1 -> x0, waiting for transfers between devices: 63.9 us -> none  [local(): lax.psum_scatter((contract_last(gate_grad, gate_weight) + contract_last(u...]
    dot_general x8 -> x0, matrix products: 25.8 us -> none  [the longest x3 11.9 us: contract_first(): lax.dot_general(first_op, second_op, (((0,), (0,)), ((), ())), preferred_...]
    unnamed x16 -> x8, local copies, waits for them, and re-layouts: 9.4 us -> 7.77 us
  transfers between devices with their start and end apart: 4 -> 0, of which waited for: 4 -> 0; matrix products, arithmetic and copies ran while one was open for 9% -> 0% of each run, Pallas kernels for 0% -> 0%
where the time goes in v1:
time: 116 us; the launch traced here: 114 us
  Pallas kernels  106 us (91%)
  local copies, waits for them, and re-layouts  7.77 us (7%)
    pallas_call x1, Pallas kernels, local(): pl.pallas_call(kernel, out_shape=(jax.ShapeDtypeStruct((16, 1024), BF), j...  106 us
    unnamed x8, local copies, waits for them, and re-layouts  7.77 us

profile of v1, /device:TPU:4, one launch (start us, length us, event | category | flops | bytes accessed | tf_op | source)
XLA Modules:
  0.0 114.1 jit_solution(9039897179319588181)
XLA Ops:
  0.6 105.7 %shard_map.84 = (bf16[16,1024]{1,0:T(8,128)(2,1)}, bf16[1024,896]{1,0:T(8,128)(2,1)}, bf16[1024,896]{1,0:T(8,128)(2,1)}, bf16[896,1024]{1,0:T(8,128)(2,1)}) custom-call(bf16[16,1024]{1,0:T(8,128)(2,1)} %x_hbm.1, bf16[16,1024]{1,0:T(8,128)(2,1)} %ct_hbm.1, bf16[1024,896]{1,0:T(8,128)(2,1)} %wg_hbm.1, bf16[1024,896]{1,0:T(8,128)(2,1)} %wu_hbm.1, ...), custom_call_target="tpu_custom_call" | custom-call | flops 7516000256 | bytes 11000000 | tf_op jit(solution)/shard_map/pallas_call | solution.py:286
  106.3 1.4 %copy.13 = bf16[16,1024]{1,0:T(8,128)(2,1)} copy(bf16[16,1024]{1,0:T(8,128)(2,1)} %get-tuple-element.8) | data formatting | bytes 65536
  107.7 0.0 copy-start.1
  107.7 3.0 %copy.14 = bf16[1024,896]{1,0:T(8,128)(2,1)} copy(bf16[1024,896]{1,0:T(8,128)(2,1)} %get-tuple-element.9) | data formatting | bytes 3670016
  110.7 0.0 copy-done.1
  110.7 0.0 copy-start
  110.7 1.2 %copy.15 = bf16[1024,896]{1,0:T(8,128)(2,1)} copy(bf16[1024,896]{1,0:T(8,128)(2,1)S(1)} %copy-done.1) | data formatting | bytes 3670016
  112.0 0.9 copy-done
  112.9 1.2 %copy.16 = bf16[896,1024]{1,0:T(8,128)(2,1)} copy(bf16[896,1024]{1,0:T(8,128)(2,1)S(1)} %copy-done) | data formatting | bytes 3670016
Async XLA Ops:
  107.7 3.0 %copy-start.1 = (bf16[1024,896]{1,0:T(8,128)(2,1)S(1)}, bf16[1024,896]{1,0:T(8,128)(2,1)}, u32[]{:S(2)}) copy-start(bf16[1024,896]{1,0:T(8,128)(2,1)} %get-tuple-element.10) | copy-start | bytes 5505028
  110.7 2.2 %copy-start = (bf16[896,1024]{1,0:T(8,128)(2,1)S(1)}, bf16[896,1024]{1,0:T(8,128)(2,1)}, u32[]{:S(2)}) copy-start(bf16[896,1024]{1,0:T(8,128)(2,1)} %get-tuple-element.11) | copy-start | bytes 5505028

commit v2 on v1

v2 whole, which is shorter than its diff:
```python
import functools

import jax
import jax.numpy as jnp
from jax import lax
from jax.experimental import pallas as pl
from jax.experimental.pallas import tpu as pltpu
from jax.sharding import PartitionSpec as P

MESH = pl.DeviceIdType.MESH
BF = jnp.bfloat16
F32 = jnp.float32
NT = (((1,), (1,)), ((), ()))
DY = (0, 1, 3, 2)
DX = (1, 3, 2)
NZ = 8
NR = 4


def kernel(
    x_hbm, ct_hbm, wg_hbm, wu_hbm, wd_hbm,
    ig_out, dwg_out, dwu_out, dwd_out,
    xb, xt, ht, wgu, wd, pt, sdn, sup, rdn, rup, gb, acc, igs, igr, ips, ipr, ilr, iys, iyr, igacc,
    w_sem, tx_s, tx_r, ty_s, ty_r, ox_s, ox_r, oy_s, oy_r, c0_s, c0_r, cc_s, cc_r,
    rs_s, rs_r, ag_s, ag_r, is_s, is_r, i0_s, i0_r, ix_s, ix_r, il_s, il_r, iy_s, iy_r,
):
    tok, z, fout = lax.axis_index("tok"), lax.axis_index("fin"), lax.axis_index("fout")
    y, x = tok // 2, (tok % 2) * 2 + fout // 2
    core = fout % 2
    me = core * 4 + x

    def at(y_, x_, c_, z_):
        return dict(tok=y_ * 2 + x_ // 2, fin=z_, fout=(x_ % 2) * 2 + c_)

    def row_peer(k):
        j = (me + k) % 8
        return at(y, j % 4, j // 4, z)

    partner = at(y, x, 1 - core, z)
    xpeer = [at(y, (x + d) % 4, core, z) for d in DX]
    ypeer = [None] + [at((y + d) % 4, x, core, z) for d in DY[1:]]
    zdn = at(y, x, core, (z + NZ - 1) % NZ)
    zup = at(y, x, core, (z + 1) % NZ)
    BACK = (0, 2, 1, 3)

    def rcopy(src, dst, ss, rs, dev):
        return pltpu.make_async_remote_copy(
            src_ref=src, dst_ref=dst, send_sem=ss, recv_sem=rs, device_id=dev, device_id_type=MESH
        )

    sends = []

    def start(copy):
        copy.start()
        sends.append(copy)

    loads = [
        pltpu.make_async_copy(x_hbm, xb.at[0, 0, me], w_sem.at[0]),
        pltpu.make_async_copy(ct_hbm, xb.at[0, 1, me], w_sem.at[1]),
        pltpu.make_async_copy(wg_hbm, wgu.at[:, 0:896], w_sem.at[2]),
        pltpu.make_async_copy(wu_hbm, wgu.at[:, 896:1792], w_sem.at[3]),
        pltpu.make_async_copy(wd_hbm, wd, w_sem.at[4]),
    ]
    for c in loads:
        c.start()

    bar = pltpu.get_barrier_semaphore()
    everyone = [row_peer(k) for k in range(1, 8)] + ypeer[1:] + [zdn, zup]
    for p in everyone:
        pl.semaphore_signal(bar, inc=1, device_id=p, device_id_type=MESH)
    pl.semaphore_wait(bar, len(everyone))

    def blk(k):
        return core * 4 + (x if k == 0 else (x + DX[k - 1]) % 4)

    def tx_send(r, i):
        return rcopy(xb.at[r, 0, me], xb.at[r, 0, me], tx_s.at[r, i], tx_r.at[r, i], xpeer[i])

    def tx_recv(r, k):
        n = BACK[k] - 1
        return rcopy(xb.at[r, 0, blk(k)], xb.at[r, 0, blk(k)], tx_s.at[r, n], tx_r.at[r, n], xpeer[k - 1])

    def ty_send(r):
        return rcopy(xb.at[0, 0, me], xb.at[BACK[r], 0, me], ty_s.at[r], ty_r.at[BACK[r]], ypeer[r])

    def ty_recv(r):
        return rcopy(xb.at[r, 0, me], xb.at[r, 0, me], ty_s.at[r], ty_r.at[r], ypeer[r])

    def ox_send(i):
        return rcopy(xb.at[0, 1, me], xb.at[0, 1, me], ox_s.at[i], ox_r.at[i], xpeer[i])

    def ox_recv(k):
        n = BACK[k] - 1
        return rcopy(xb.at[0, 1, blk(k)], xb.at[0, 1, blk(k)], ox_s.at[n], ox_r.at[n], xpeer[k - 1])

    def oy_send(r, k):
        q = BACK[r]
        return rcopy(xb.at[0, 1, blk(k)], xb.at[q, 1, blk(k)], oy_s.at[r, k], oy_r.at[q, k], ypeer[r])

    def oy_recv(r, k):
        return rcopy(xb.at[r, 1, blk(k)], xb.at[r, 1, blk(k)], oy_s.at[r, k], oy_r.at[r, k], ypeer[r])

    def c0_copy(a, k, own=True):
        b = blk(k) if own else (4 - 4 * core) + blk(k) - 4 * core
        return rcopy(xb.at[0, a, b], xb.at[0, a, b], c0_s.at[a, k], c0_r.at[a, k], partner)

    def cc_copy(r, a, own=True):
        b = pl.ds(4 * core if own else 4 - 4 * core, 4)
        return rcopy(xb.at[r, a, b], xb.at[r, a, b], cc_s.at[r, a], cc_r.at[r, a], partner)

    def own_sends():
        loads[0].wait()
        for i in range(3):
            start(tx_send(0, i))
        start(c0_copy(0, 0))
        start(ty_send(1))
        loads[1].wait()
        for i in range(3):
            start(ox_send(i))
        start(c0_copy(1, 0))
        start(oy_send(1, 0))
        start(ty_send(2))
        start(oy_send(2, 0))

    def tok_in():
        for k in (1, 2, 3):
            tx_recv(0, k).wait_recv()
            start(c0_copy(0, k))

    def forward_y(r):
        ty_recv(r).wait_recv()
        for i in range(3):
            start(tx_send(r, i))

    def cot_in():
        for k in (1, 2, 3):
            ox_recv(k).wait_recv()
            start(c0_copy(1, k))
            start(oy_send(1, k))

    def send_y(r):
        if r == 2:
            for k in (1, 2, 3):
                start(oy_send(2, k))
        else:
            start(ty_send(3))
            for k in range(4):
                start(oy_send(3, k))

    nd = [4, 3, 4, 3]

    def hand_over(r):
        for k in (1, 2, 3):
            tx_recv(r, k).wait_recv()
        start(cc_copy(r, 0))
        for k in (0, 1, 2, 3):
            oy_recv(r, k).wait_recv()
        start(cc_copy(r, 1))

    def partials(r):
        if r == 0:
            for k in range(4):
                c0_copy(0, k, False).wait_recv()
            loads[2].wait()
            loads[3].wait()
        else:
            cc_copy(r, 0, False).wait_recv()
        toks = xb[r, 0].reshape(128, 1024)
        both = jnp.dot(toks, wgu[...], preferred_element_type=F32)
        pt[r, :, 0] = both[:, :896].reshape(8, 16, 896)
        pt[r, :, 1] = both[:, 896:].reshape(8, 16, 896)
        if r == 0:
            for k in range(4):
                c0_copy(1, k, False).wait_recv()
            loads[4].wait()
        else:
            cc_copy(r, 1, False).wait_recv()
        cots = xb[r, 1].reshape(128, 1024)
        pt[r, :, 2] = lax.dot_general(cots, wd[...], NT, preferred_element_type=F32).reshape(8, 16, 896)
        send_sums(r, 0)
        xt[r // 2, :, (r % 2) * 128:(r % 2) * 128 + 128] = toks.T

    def dn_copy(r, s):
        return rcopy(sdn.at[r, s], rdn.at[r, s], rs_s.at[r, 0, s], rs_r.at[r, 0, s], zdn)

    def up_copy(r, s):
        return rcopy(sup.at[r, s], rup.at[r, s], rs_s.at[r, 1, s], rs_r.at[r, 1, s], zup)

    def send_sums(r, s):
        n, m = nd[r], 7 - nd[r]
        if s < n:
            mine = pt[r, (z - n + s + NZ) % NZ]
            if s > 0:
                dn_copy(r, s - 1).wait_recv()
                mine = mine + rdn[r, s - 1].astype(F32)
            sdn[r, s] = mine.astype(BF)
            start(dn_copy(r, s))
        if s < m:
            mine = pt[r, (z + m - s) % NZ]
            if s > 0:
                up_copy(r, s - 1).wait_recv()
                mine = mine + rup[r, s - 1].astype(F32)
            sup[r, s] = mine.astype(BF)
            start(up_copy(r, s))

    def ag_copy(r, d, t, recv=False):
        t_ = t + 1 if recv else t
        c = (z + t_) % NZ if d == 0 else (z - t_ + NZ) % NZ
        return rcopy(gb.at[r, c], gb.at[r, c], ag_s.at[r, d, t], ag_r.at[r, d, t], zdn if d == 0 else zup)

    def act(r):
        n, m = nd[r], 7 - nd[r]
        dn_copy(r, n - 1).wait_recv()
        up_copy(r, m - 1).wait_recv()
        total = pt[r, z] + rdn[r, n - 1].astype(F32) + rup[r, m - 1].astype(F32)
        g, u, hg = total[0], total[1], total[2]
        s = jax.nn.sigmoid(g)
        silu = g * s
        gb[r, z, 2] = (silu * u).astype(BF)
        gb[r, z, 0] = (hg * u * s * (1.0 + g * (1.0 - s))).astype(BF)
        gb[r, z, 1] = (hg * silu).astype(BF)

    def spread(r, t):
        hops = (7 - nd[r], nd[r])
        for d in (0, 1):
            if 0 < t <= hops[d]:
                ag_copy(r, d, t - 1, True).wait_recv()
            if t < hops[d]:
                start(ag_copy(r, d, t))

    def stage(r, s):
        if s < 4:
            send_sums(r, s)
        else:
            if s == 4:
                act(r)
            spread(r, s - 4)

    def pr_copy(r):
        b = pl.ds(4 - 4 * core, 4)
        return rcopy(igs.at[r, b], igr.at[r], is_s.at[r], is_r.at[r], partner)

    def p0_copy(i):
        return rcopy(igs.at[0, 4 - 4 * core + i], igr.at[0, i], i0_s.at[i], i0_r.at[i], partner)

    def px_copy(r, n):
        m = BACK[n + 1] - 1
        return rcopy(ips.at[r, (x + DX[n]) % 4], ipr.at[r, m], ix_s.at[r, n], ix_r.at[r, m], xpeer[n])

    def px_recv(r, n):
        return rcopy(ips.at[r, 0], ipr.at[r, n], ix_s.at[r, n], ix_r.at[r, n], xpeer[n])

    far = (z + 4) % NZ

    def late_copy():
        n = (me - far + 8) % 8
        return rcopy(igs.at[0, far], ilr.at[n], il_s.at[0], il_r.at[n], at(y, far % 4, far // 4, z))

    def late_recv(n):
        return rcopy(igs.at[0, 0], ilr.at[n], il_s.at[0], il_r.at[n], row_peer(n))

    def input_rows(r, chunks):
        both = jnp.concatenate(
            [jnp.concatenate([gb[r, c, 0], gb[r, c, 1]], axis=1) for c in chunks], axis=0
        )
        part = lax.dot_general(both, wgu[...], NT, preferred_element_type=F32).astype(BF)
        for n, c in enumerate(chunks):
            igs[r, c] = part[16 * n:16 * n + 16]

    def input_part(r):
        input_rows(r, range(8))
        start(pr_copy(r))

    def pair_sum(r):
        pr_copy(r).wait_recv()
        own = igs[r, pl.ds(4 * core, 4)]
        ips[r] = (own.astype(F32) + igr[r].astype(F32)).astype(BF)
        for n in range(3):
            start(px_copy(r, n))

    def input_early():
        input_rows(0, [(z + n + NZ) % NZ for n in range(-3, 4)])
        for i in range(4):

            @pl.when(4 - 4 * core + i != far)
            def _(i=i):
                p0_copy(i).start()

    def pair_early():
        for n in range(4):
            i = (x + ((0,) + DX)[n]) % 4

            @pl.when(4 * core + i != far)
            def _(i=i, n=n):
                p0_copy(i).wait_recv()
                own = igs[0, 4 * core + i]
                ips[0, i] = (own.astype(F32) + igr[0, i].astype(F32)).astype(BF)
                if n > 0:
                    px_copy(0, n - 1).start()

    def input_late():
        input_rows(0, [far])

        @pl.when(me != far)
        def _():
            late_copy().start()

    def add_dw(p, i, lhs, rhs, out, first):
        width = rhs.shape[1]
        for c in range(0, width, 256):
            e = min(c + 256, width)
            v = jnp.dot(lhs, rhs[:, c:e], preferred_element_type=F32)
            if first:
                acc[i, :lhs.shape[0], c:e] = v
            else:
                out[:, c:e] = (acc[i, :lhs.shape[0], c:e] + v).astype(BF)

    def weights_part(p, first):
        rs = slice(2 * p, 2 * p + 2)
        add_dw(p, 0, xt[p], gb[rs, :, 0].reshape(256, 896), dwg_out, first)
        add_dw(p, 1, xt[p], gb[rs, :, 1].reshape(256, 896), dwu_out, first)
        ht[...] = gb[rs, :, 2].reshape(256, 896).T
        add_dw(p, 2, ht[...], xb[rs, 1].reshape(256, 1024), dwd_out, first)

    def iy_copy(r):
        return rcopy(iys.at[r], iyr.at[r], iy_s.at[r], iy_r.at[r], ypeer[r])

    def row_sum(r):
        v = ips[r, x].astype(F32)
        for n in range(3):
            px_recv(r, n).wait_recv()
            v = v + ipr[r, n].astype(F32)
        iys[r] = v.astype(BF)
        start(iy_copy(r))

    def finish():
        @pl.when(me != far)
        def _():
            v = ips[0, x].astype(F32)
            for n in range(3):
                px_recv(0, n).wait_recv()
                v = v + ipr[0, n].astype(F32)
            igacc[...] = v

        @pl.when(me == far)
        def _():
            v = igs[0, me].astype(F32)
            for n in range(1, 8):
                late_recv(n).wait_recv()
                v = v + ilr[n].astype(F32)
            igacc[...] = v

        total = igacc[...]
        for r in (1, 2, 3):
            iy_copy(r).wait_recv()
            total = total + iyr[r].astype(F32)
        ig_out[...] = total.astype(BF)
        for i in range(4):

            @pl.when(4 - 4 * core + i != far)
            def _(i=i):
                p0_copy(i).wait_send()

        for n in range(3):

            @pl.when(4 * core + (x + DX[n]) % 4 != far)
            def _(n=n):
                px_copy(0, n).wait_send()

        @pl.when(me != far)
        def _():
            late_copy().wait_send()

    steps = []

    def then(fn, *given):
        steps.append((fn, given))

    then(own_sends)
    then(tok_in)
    then(forward_y, 1)
    then(cot_in)
    then(partials, 0)
    then(forward_y, 2)
    then(send_y, 2)
    then(hand_over, 1)
    then(partials, 1)
    then(send_y, 3)
    then(hand_over, 2)
    then(stage, 0, 1)
    then(partials, 2)
    then(stage, 1, 1)
    then(forward_y, 3)
    then(stage, 0, 2)
    then(stage, 2, 1)
    then(hand_over, 3)
    then(stage, 1, 2)
    then(partials, 3)
    for s in range(3, 9):
        then(stage, 1, s)
        then(stage, 2, s - 1)
        then(stage, 3, s - 2)
        if s > 5:
            then(stage, 0, s - 3)
    then(input_part, 1)
    then(stage, 2, 8)
    then(stage, 3, 7)
    then(stage, 0, 6)
    then(input_part, 2)
    then(pair_sum, 1)
    then(stage, 0, 7)
    then(stage, 3, 8)
    then(input_part, 3)
    then(pair_sum, 2)
    then(input_early)
    then(row_sum, 1)
    then(pair_sum, 3)
    then(row_sum, 2)
    then(pair_early)
    then(weights_part, 1, True)
    then(stage, 0, 8)
    then(input_late)
    then(row_sum, 3)
    then(weights_part, 0, False)
    then(finish)
    for fn, given in steps:
        fn(*given)
    for c in sends:
        c.wait_send()


def writer(*refs):
    sem = refs[8]
    copies = [pltpu.make_async_copy(refs[i], refs[4 + i], sem.at[i]) for i in range(4)]
    for c in copies:
        c.start()
    for c in copies:
        c.wait()


def local(tokens_in, cotangent, gate_weight, up_weight, down_weight):
    vm = pltpu.VMEM
    dma = pltpu.SemaphoreType.DMA
    outs = pl.pallas_call(
        kernel,
        out_shape=(
            pltpu.VMEM((16, 1024), BF),
            pltpu.VMEM((1024, 896), BF),
            pltpu.VMEM((1024, 896), BF),
            pltpu.VMEM((896, 1024), BF),
        ),
        in_specs=[pl.BlockSpec(memory_space=pl.ANY)] * 5,
        out_specs=[pl.BlockSpec(memory_space=pltpu.VMEM)] * 4,
        scratch_shapes=[
            vm((4, 2, 8, 16, 1024), BF),
            vm((2, 1024, 256), BF),
            vm((896, 256), BF),
            vm((1024, 1792), BF),
            vm((896, 1024), BF),
            vm((4, 8, 3, 16, 896), F32),
            vm((4, 4, 3, 16, 896), BF),
            vm((4, 4, 3, 16, 896), BF),
            vm((4, 4, 3, 16, 896), BF),
            vm((4, 4, 3, 16, 896), BF),
            vm((4, 8, 3, 16, 896), BF),
            vm((3, 1024, 1024), F32),
            vm((4, 8, 16, 1024), BF),
            vm((4, 4, 16, 1024), BF),
            vm((4, 4, 16, 1024), BF),
            vm((4, 3, 16, 1024), BF),
            vm((8, 16, 1024), BF),
            vm((4, 16, 1024), BF),
            vm((4, 16, 1024), BF),
            vm((16, 1024), F32),
            dma((5,)),
            dma((4, 3)), dma((4, 3)),
            dma((4,)), dma((4,)),
            dma((3,)), dma((3,)),
            dma((4, 4)), dma((4, 4)),
            dma((2, 4)), dma((2, 4)),
            dma((4, 2)), dma((4, 2)),
            dma((4, 2, 4)), dma((4, 2, 4)),
            dma((4, 2, 4)), dma((4, 2, 4)),
            dma((4,)), dma((4,)),
            dma((4,)), dma((4,)),
            dma((4, 3)), dma((4, 3)),
            dma((1,)), dma((8,)),
            dma((4,)), dma((4,)),
        ],
        compiler_params=pltpu.CompilerParams(
            collective_id=0, has_side_effects=True, vmem_limit_bytes=48 * 2**20
        ),
        cost_estimate=pl.CostEstimate(flops=7_516_000_000, bytes_accessed=11_000_000, transcendentals=0),
    )(tokens_in, cotangent, gate_weight, up_weight, down_weight)
    outs = [pltpu.with_memory_space_constraint(a, pltpu.MemorySpace.VMEM) for a in outs]
    return pl.pallas_call(
        writer,
        out_shape=(
            jax.ShapeDtypeStruct((16, 1024), BF),
            jax.ShapeDtypeStruct((1024, 896), BF),
            jax.ShapeDtypeStruct((1024, 896), BF),
            jax.ShapeDtypeStruct((896, 1024), BF),
        ),
        in_specs=[pl.BlockSpec(memory_space=pltpu.VMEM)] * 4,
        out_specs=[pl.BlockSpec(memory_space=pl.ANY)] * 4,
        scratch_shapes=[pltpu.SemaphoreType.DMA((4,))],
        compiler_params=pltpu.CompilerParams(vmem_limit_bytes=2**20),
        cost_estimate=pl.CostEstimate(flops=0, bytes_accessed=11_000_000, transcendentals=0),
    )(*outs)


def solution(mesh):
    in_specs = (
        P(("tok", "fout"), "fin"),
        P(("tok", "fout"), "fin"),
        P("fin", ("tok", "fout")),
        P("fin", ("tok", "fout")),
        P(("tok", "fout"), "fin"),
    )
    out_specs = (
        P(("tok", "fout"), "fin"),
        P("fin", ("tok", "fout")),
        P("fin", ("tok", "fout")),
        P(("tok", "fout"), "fin"),
    )
    return jax.shard_map(local, mesh=mesh, in_specs=in_specs, out_specs=out_specs, check_vma=False)
```

time: 116 us -> 97.9 us (0.84)
  Pallas kernels: 106 us -> 93.7 us
  local copies, waits for them, and re-layouts: 7.77 us -> 1.51 us
    pallas_call x1 -> x2, Pallas kernels: 106 us -> 93.7 us  [the longest x1 91.2 us: local(): pl.pallas_call(kernel, out_shape=(pltpu.VMEM((16, 1024), BF), pltpu.VMEM(...]
    unnamed x8 -> x4, local copies, waits for them, and re-layouts: 7.77 us -> 1.51 us
where the time goes in v2:
time: 97.9 us; the launch traced here: 96 us
  Pallas kernels  93.7 us (96%)
  local copies, waits for them, and re-layouts  1.51 us (2%)
    pallas_call x1, Pallas kernels, local(): pl.pallas_call(kernel, out_shape=(pltpu.VMEM((16, 1024), BF), pltpu.VMEM(...  91.2 us
    pallas_call x1, Pallas kernels, local(): pl.pallas_call(writer, out_shape=(jax.ShapeDtypeStruct((16, 1024), BF), j...  2.48 us

profile of v2, /device:TPU:4, one launch (start us, length us, event | category | flops | bytes accessed | tf_op | source)
XLA Modules:
  0.0 96.0 jit_solution(18335810603909858974)
XLA Ops:
  0.6 0.0 copy-start
  0.6 0.7 copy-done
  1.4 0.0 copy-start.1
  1.4 0.8 copy-done.1
  2.1 91.2 %shard_map.84 = (bf16[16,1024]{1,0:T(8,128)(2,1)S(1)}, bf16[1024,896]{1,0:T(8,128)(2,1)S(1)}, bf16[1024,896]{1,0:T(8,128)(2,1)S(1)}, bf16[896,1024]{1,0:T(8,128)(2,1)S(1)}) custom-call(bf16[16,1024]{1,0:T(8,128)(2,1)S(1)} %copy-done, bf16[16,1024]{1,0:T(8,128)(2,1)S(1)} %copy-done.1, bf16[1024,896]{1,0:T(8,128)(2,1)} %wg_hbm.1, bf16[1024,896]{1,0:T(8,128)(2,1)} %wu_hbm.1, ...), custom_call_target="tpu_custom_call" | custom-call | flops 7516000256 | bytes 11000000 | tf_op jit(solution)/shard_map/pallas_call | solution.py:444
  93.4 2.5 %shard_map.85 = (bf16[16,1024]{1,0:T(8,128)(2,1)}, bf16[1024,896]{1,0:T(8,128)(2,1)}, bf16[1024,896]{1,0:T(8,128)(2,1)}, bf16[896,1024]{1,0:T(8,128)(2,1)}) custom-call(bf16[16,1024]{1,0:T(8,128)(2,1)S(1)} %get-tuple-element.8.refs_0_, bf16[1024,896]{1,0:T(8,128)(2,1)S(1)} %get-tuple-element.9.refs_1_, bf16[1024,896]{1,0:T(8,128)(2,1)S(1)} %get-tuple-element.10.refs_2_, ...), custom_call_target="tpu_custom_call" | custom-call | bytes 11000000 | tf_op jit(solution)/shard_map/pallas_call | solution.py:496
Async XLA Ops:
  0.6 0.8 copy-start
  1.4 0.8 copy-start.1

commit v3 on v2

v3 whole, which is shorter than its diff:
```python
import functools

import jax
import jax.numpy as jnp
from jax import lax
from jax.experimental import pallas as pl
from jax.experimental.pallas import tpu as pltpu
from jax.sharding import PartitionSpec as P

MESH = pl.DeviceIdType.MESH
BF = jnp.bfloat16
F32 = jnp.float32
NT = (((1,), (1,)), ((), ()))
DY = (0, 1, 3, 2)
DX = (1, 3, 2)
NZ = 8
NR = 4


def kernel(
    x_hbm, ct_hbm, wg_hbm, wu_hbm, wd_hbm,
    ig_out, dwg_out, dwu_out, dwd_out,
    xb, xt, ht, wgu, wd, pt, sdn, sup, rdn, rup, gb, igs, igr, ips, ipr, ils, ilr, iys, iyr, igacc,
    w_sem, g_s, g_r, c0_s, c0_r, cc_s, cc_r,
    rs_s, rs_r, ag_s, ag_r, i0_s, i0_r, ix_s, ix_r, il_s, il_r, iy_s, iy_r,
):
    tok, z, fout = lax.axis_index("tok"), lax.axis_index("fin"), lax.axis_index("fout")
    y, x = tok // 2, (tok % 2) * 2 + fout // 2
    core = fout % 2
    me = core * 4 + x

    def at(y_, x_, c_, z_):
        return dict(tok=y_ * 2 + x_ // 2, fin=z_, fout=(x_ % 2) * 2 + c_)

    def row_peer(k):
        j = (me + k) % 8
        return at(y, j % 4, j // 4, z)

    partner = at(y, x, 1 - core, z)
    xpeer = [at(y, (x + d) % 4, core, z) for d in DX]
    ypeer = [None] + [at((y + d) % 4, x, core, z) for d in DY[1:]]
    zdn = at(y, x, core, (z + NZ - 1) % NZ)
    zup = at(y, x, core, (z + 1) % NZ)
    BACK = (0, 2, 1, 3)

    def rcopy(src, dst, ss, rs, dev):
        return pltpu.make_async_remote_copy(
            src_ref=src, dst_ref=dst, send_sem=ss, recv_sem=rs, device_id=dev, device_id_type=MESH
        )

    sends = []

    def start(copy):
        copy.start()
        sends.append(copy)

    loads = [
        pltpu.make_async_copy(x_hbm, xb.at[0, 0, me], w_sem.at[0]),
        pltpu.make_async_copy(ct_hbm, xb.at[0, 1, me], w_sem.at[1]),
        pltpu.make_async_copy(wg_hbm, wgu.at[:, 0:896], w_sem.at[2]),
        pltpu.make_async_copy(wu_hbm, wgu.at[:, 896:1792], w_sem.at[3]),
        pltpu.make_async_copy(wd_hbm, wd, w_sem.at[4]),
    ]
    for c in loads:
        c.start()

    bar = pltpu.get_barrier_semaphore()
    everyone = [row_peer(k) for k in range(1, 8)] + ypeer[1:] + [zdn, zup]
    for p in everyone:
        pl.semaphore_signal(bar, inc=1, device_id=p, device_id_type=MESH)
    far = [(z + 4 + 2 * r) % NZ for r in range(4)]
    for r in range(4):

        @pl.when(me == far[r])
        def _(r=r):
            for n in range(1 if r == 0 else 0, 8):
                j = (me + n) % 8
                source = at((y + 4 - DY[r]) % 4, j % 4, j // 4, z)
                pl.semaphore_signal(bar, inc=1, device_id=source, device_id_type=MESH)

    pl.semaphore_wait(bar, len(everyone) + jnp.where(me == far[0], 3, 4))

    def blk(k):
        return core * 4 + (x if k == 0 else (x + DX[k - 1]) % 4)

    def x_send(r, a, k):
        return rcopy(xb.at[r, a, me], xb.at[r, a, me], g_s.at[r, a, k], g_r.at[r, a, BACK[k]], xpeer[k - 1])

    def y_send(r, a, k):
        q = BACK[r]
        return rcopy(xb.at[0, a, blk(k)], xb.at[q, a, blk(k)], g_s.at[r, a, k], g_r.at[q, a, k], ypeer[r])

    def g_recv(r, a, k):
        dev = xpeer[k - 1] if r in (0, 3) and k > 0 else ypeer[r]
        return rcopy(xb.at[r, a, blk(k)], xb.at[r, a, blk(k)], g_s.at[r, a, k], g_r.at[r, a, k], dev)

    def c0_copy(a, k, own=True):
        b = blk(k) if own else (4 - 4 * core) + blk(k) - 4 * core
        return rcopy(xb.at[0, a, b], xb.at[0, a, b], c0_s.at[a, k], c0_r.at[a, k], partner)

    def cc_copy(r, a, own=True):
        b = pl.ds(4 * core if own else 4 - 4 * core, 4)
        return rcopy(xb.at[r, a, b], xb.at[r, a, b], cc_s.at[r, a], cc_r.at[r, a], partner)

    def own_sends():
        for a in (0, 1):
            loads[a].wait()
            for k in (1, 2, 3):
                start(x_send(0, a, k))
            start(c0_copy(a, 0))
            start(y_send(1, a, 0))
            start(y_send(2, a, 0))
        for a in (0, 1):
            start(y_send(3, a, 0))

    def row_in(a):
        for k in (1, 2, 3):
            g_recv(0, a, k).wait_recv()
            start(c0_copy(a, k))
            start(y_send(1, a, k))
            start(y_send(2, a, k))

    def third_in(a):
        g_recv(3, a, 0).wait_recv()
        for k in (1, 2, 3):
            start(x_send(3, a, k))

    nd = [4, 3, 4, 3]

    def hand_over(r):
        for a in (0, 1):
            for k in range(4):
                if r != 3 or k > 0:
                    g_recv(r, a, k).wait_recv()
            start(cc_copy(r, a))

    def partials(r):
        if r == 0:
            for k in range(4):
                c0_copy(0, k, False).wait_recv()
            loads[2].wait()
            loads[3].wait()
        else:
            cc_copy(r, 0, False).wait_recv()
        toks = xb[r, 0].reshape(128, 1024)
        both = jnp.dot(toks, wgu[...], preferred_element_type=F32)
        pt[r, :, 0] = both[:, :896].reshape(8, 16, 896)
        pt[r, :, 1] = both[:, 896:].reshape(8, 16, 896)
        if r == 0:
            for k in range(4):
                c0_copy(1, k, False).wait_recv()
            loads[4].wait()
        else:
            cc_copy(r, 1, False).wait_recv()
        cots = xb[r, 1].reshape(128, 1024)
        pt[r, :, 2] = lax.dot_general(cots, wd[...], NT, preferred_element_type=F32).reshape(8, 16, 896)
        send_sums(r, 0)
        xt[:, r * 128:r * 128 + 128] = toks.T

    def dn_copy(r, s):
        return rcopy(sdn.at[r, s], rdn.at[r, s], rs_s.at[r, 0, s], rs_r.at[r, 0, s], zdn)

    def up_copy(r, s):
        return rcopy(sup.at[r, s], rup.at[r, s], rs_s.at[r, 1, s], rs_r.at[r, 1, s], zup)

    def send_sums(r, s):
        n, m = nd[r], 7 - nd[r]
        if s < n:
            mine = pt[r, (z - n + s + NZ + 2 * r) % NZ]
            if s > 0:
                dn_copy(r, s - 1).wait_recv()
                mine = mine + rdn[r, s - 1].astype(F32)
            sdn[r, s] = mine.astype(BF)
            start(dn_copy(r, s))
        if s < m:
            mine = pt[r, (z + m - s + 2 * r) % NZ]
            if s > 0:
                up_copy(r, s - 1).wait_recv()
                mine = mine + rup[r, s - 1].astype(F32)
            sup[r, s] = mine.astype(BF)
            start(up_copy(r, s))

    def ag_copy(r, d, t, recv=False):
        t_ = t + 1 if recv else t
        c = (z + t_ + 2 * r) % NZ if d == 0 else (z - t_ + NZ + 2 * r) % NZ
        return rcopy(gb.at[r, c], gb.at[r, c], ag_s.at[r, d, t], ag_r.at[r, d, t], zdn if d == 0 else zup)

    def act(r):
        n, m = nd[r], 7 - nd[r]
        dn_copy(r, n - 1).wait_recv()
        up_copy(r, m - 1).wait_recv()
        own = (z + 2 * r) % NZ
        total = pt[r, own] + rdn[r, n - 1].astype(F32) + rup[r, m - 1].astype(F32)
        g, u, hg = total[0], total[1], total[2]
        s = jax.nn.sigmoid(g)
        silu = g * s
        gb[r, own, 2] = (silu * u).astype(BF)
        gb[r, own, 0] = (hg * u * s * (1.0 + g * (1.0 - s))).astype(BF)
        gb[r, own, 1] = (hg * silu).astype(BF)

    def spread(r, t):
        hops = (7 - nd[r], nd[r])
        for d in (0, 1):
            if 0 < t <= hops[d]:
                ag_copy(r, d, t - 1, True).wait_recv()
            if t < hops[d]:
                start(ag_copy(r, d, t))

    def stage(r, s):
        if s < 4:
            send_sums(r, s)
        else:
            if s == 4:
                act(r)
            spread(r, s - 4)

    def p0_copy(r, i):
        return rcopy(igs.at[r, 4 - 4 * core + i], igr.at[r, i], i0_s.at[r, i], i0_r.at[r, i], partner)

    def px_copy(r, n):
        m = BACK[n + 1] - 1
        return rcopy(ips.at[r, (x + DX[n]) % 4], ipr.at[r, m], ix_s.at[r, n], ix_r.at[r, m], xpeer[n])

    def px_recv(r, n):
        return rcopy(ips.at[r, 0], ipr.at[r, n], ix_s.at[r, n], ix_r.at[r, n], xpeer[n])

    def late_copy(r):
        owner = at((y + DY[r]) % 4, far[r] % 4, far[r] // 4, z)
        n = (me - far[r] + 8) % 8
        return rcopy(ils.at[r], ilr.at[n], il_s.at[r], il_r.at[n], owner)

    def late_recv(n):
        return rcopy(ils.at[0], ilr.at[n], il_s.at[0], il_r.at[n], partner)

    def input_rows(chunks):
        both = jnp.concatenate(
            [jnp.concatenate([gb[r, c, 0], gb[r, c, 1]], axis=1) for r, c in chunks], axis=0
        )
        return lax.dot_general(both, wgu[...], NT, preferred_element_type=F32).astype(BF)

    def input_early(r):
        chunks = [(r, (z + n + NZ + 2 * r) % NZ) for n in range(-3, 4)]
        part = input_rows(chunks)
        for n, (_, c) in enumerate(chunks):
            igs[r, c] = part[16 * n:16 * n + 16]
        for i in range(4):

            @pl.when(4 - 4 * core + i != far[r])
            def _(i=i):
                p0_copy(r, i).start()

    def pair_early(r):
        for n in range(4):
            i = (x + ((0,) + DX)[n]) % 4

            @pl.when(4 * core + i != far[r])
            def _(i=i, n=n):
                p0_copy(r, i).wait_recv()
                own = igs[r, 4 * core + i]
                ips[r, i] = (own.astype(F32) + igr[r, i].astype(F32)).astype(BF)
                if n > 0:
                    px_copy(r, n - 1).start()

    def input_late():
        part = input_rows([(r, far[r]) for r in range(4)])
        for r in range(4):
            ils[r] = part[16 * r:16 * r + 16]
            if r > 0:
                start(late_copy(r))

        @pl.when(me != far[0])
        def _():
            late_copy(0).start()

    def row_total(r):
        v = ips[r, x].astype(F32)
        for n in range(3):
            px_recv(r, n).wait_recv()
            v = v + ipr[r, n].astype(F32)
        return v

    def row_sum(r):
        @pl.when(me != far[r])
        def _():
            iys[r] = row_total(r).astype(BF)
            iy_copy(r).start()

    def early_end(r):
        for i in range(4):

            @pl.when(4 - 4 * core + i != far[r])
            def _(i=i):
                p0_copy(r, i).wait_send()

        for n in range(3):

            @pl.when(4 * core + (x + DX[n]) % 4 != far[r])
            def _(n=n):
                px_copy(r, n).wait_send()

        @pl.when(me != far[r])
        def _():
            if r == 0:
                late_copy(0).wait_send()
            else:
                iy_copy(r).wait_send()

    def add_dw(lhs, rhs, out):
        width = rhs.shape[1]
        for c in range(0, width, 256):
            e = min(c + 256, width)
            out[:, c:e] = jnp.dot(lhs[...], rhs[:, c:e], preferred_element_type=F32).astype(BF)

    def turn_hidden(r):
        ht[:, r * 128:r * 128 + 128] = gb[r, :, 2].reshape(128, 896).T

    def weights_part(n):
        if n < 2:
            add_dw(xt, gb[:, :, n].reshape(512, 896), (dwg_out, dwu_out)[n])
        else:
            add_dw(ht, xb[:, 1].reshape(512, 1024), dwd_out)

    def iy_copy(r):
        return rcopy(iys.at[r], iyr.at[r], iy_s.at[r], iy_r.at[r], ypeer[r])

    def finish():
        igacc[...] = jnp.zeros_like(igacc)
        for r in (3, 2, 1, 0):

            @pl.when(me != far[r])
            def _(r=r):
                if r == 0:
                    igacc[...] += row_total(0)
                else:
                    iy_copy(r).wait_recv()
                    igacc[...] += iyr[r].astype(F32)

        for r in range(4):

            @pl.when(me == far[r])
            def _(r=r):
                v = igacc[...]
                if r == 0:
                    v = v + ils[0].astype(F32)
                for n in range(1 if r == 0 else 0, 8):
                    late_recv(n).wait_recv()
                    v = v + ilr[n].astype(F32)
                igacc[...] = v

        ig_out[...] = igacc[...].astype(BF)
        for r in range(4):
            early_end(r)

    steps = []

    def then(fn, *given):
        steps.append((fn, given))

    then(own_sends)
    then(row_in, 0)
    then(row_in, 1)
    then(third_in, 0)
    then(third_in, 1)
    then(partials, 0)
    then(hand_over, 1)
    then(hand_over, 2)
    then(partials, 1)
    then(partials, 2)
    then(stage, 0, 1)
    then(hand_over, 3)
    then(partials, 3)
    then(stage, 1, 1)
    then(stage, 2, 1)
    then(stage, 0, 2)
    done, last = [2, 1, 1, 0], [2, 0]
    while min(done) < 6:
        free = [q for q in (3, 2, 1, 0) if q not in last[-2:] and done[q] < 6]
        r = min(free or (3, 2, 1, 0), key=lambda q: done[q])
        done[r] += 1
        last.append(r)
        then(stage, r, done[r])
    then(stage, 3, 7)
    then(input_early, 3)
    then(stage, 2, 7)
    then(input_early, 2)
    then(pair_early, 3)
    then(stage, 1, 7)
    then(input_early, 1)
    then(pair_early, 2)
    then(stage, 0, 7)
    then(input_early, 0)
    then(pair_early, 1)
    for r in (3, 2, 1, 0):
        then(stage, r, 8)
    then(input_late)
    then(pair_early, 0)
    for r in range(4):
        then(turn_hidden, r)
    then(row_sum, 3)
    then(row_sum, 2)
    then(row_sum, 1)
    for n in range(3):
        then(weights_part, n)
    then(finish)
    for fn, given in steps:
        fn(*given)
    for c in sends:
        c.wait_send()


def writer(*refs):
    sem = refs[8]
    copies = [pltpu.make_async_copy(refs[i], refs[4 + i], sem.at[i]) for i in range(4)]
    for c in copies:
        c.start()
    for c in copies:
        c.wait()


def local(tokens_in, cotangent, gate_weight, up_weight, down_weight):
    vm = pltpu.VMEM
    dma = pltpu.SemaphoreType.DMA
    outs = pl.pallas_call(
        kernel,
        out_shape=(
            pltpu.VMEM((16, 1024), BF),
            pltpu.VMEM((1024, 896), BF),
            pltpu.VMEM((1024, 896), BF),
            pltpu.VMEM((896, 1024), BF),
        ),
        in_specs=[pl.BlockSpec(memory_space=pl.ANY)] * 5,
        out_specs=[pl.BlockSpec(memory_space=pltpu.VMEM)] * 4,
        scratch_shapes=[
            vm((4, 2, 8, 16, 1024), BF),
            vm((1024, 512), BF),
            vm((896, 512), BF),
            vm((1024, 1792), BF),
            vm((896, 1024), BF),
            vm((4, 8, 3, 16, 896), F32),
            vm((4, 4, 3, 16, 896), BF),
            vm((4, 4, 3, 16, 896), BF),
            vm((4, 4, 3, 16, 896), BF),
            vm((4, 4, 3, 16, 896), BF),
            vm((4, 8, 3, 16, 896), BF),
            vm((4, 8, 16, 1024), BF),
            vm((4, 4, 16, 1024), BF),
            vm((4, 4, 16, 1024), BF),
            vm((4, 3, 16, 1024), BF),
            vm((4, 16, 1024), BF),
            vm((8, 16, 1024), BF),
            vm((4, 16, 1024), BF),
            vm((4, 16, 1024), BF),
            vm((16, 1024), F32),
            dma((5,)),
            dma((4, 2, 4)), dma((4, 2, 4)),
            dma((2, 4)), dma((2, 4)),
            dma((4, 2)), dma((4, 2)),
            dma((4, 2, 4)), dma((4, 2, 4)),
            dma((4, 2, 4)), dma((4, 2, 4)),
            dma((4, 4)), dma((4, 4)),
            dma((4, 3)), dma((4, 3)),
            dma((4,)), dma((8,)),
            dma((4,)), dma((4,)),
        ],
        compiler_params=pltpu.CompilerParams(
            collective_id=0, has_side_effects=True, vmem_limit_bytes=48 * 2**20
        ),
        cost_estimate=pl.CostEstimate(flops=7_516_000_000, bytes_accessed=11_000_000, transcendentals=0),
    )(tokens_in, cotangent, gate_weight, up_weight, down_weight)
    outs = [pltpu.with_memory_space_constraint(a, pltpu.MemorySpace.VMEM) for a in outs]
    return pl.pallas_call(
        writer,
        out_shape=(
            jax.ShapeDtypeStruct((16, 1024), BF),
            jax.ShapeDtypeStruct((1024, 896), BF),
            jax.ShapeDtypeStruct((1024, 896), BF),
            jax.ShapeDtypeStruct((896, 1024), BF),
        ),
        in_specs=[pl.BlockSpec(memory_space=pltpu.VMEM)] * 4,
        out_specs=[pl.BlockSpec(memory_space=pl.ANY)] * 4,
        scratch_shapes=[pltpu.SemaphoreType.DMA((4,))],
        compiler_params=pltpu.CompilerParams(vmem_limit_bytes=2**20),
        cost_estimate=pl.CostEstimate(flops=0, bytes_accessed=11_000_000, transcendentals=0),
    )(*outs)


def solution(mesh):
    in_specs = (
        P(("tok", "fout"), "fin"),
        P(("tok", "fout"), "fin"),
        P("fin", ("tok", "fout")),
        P("fin", ("tok", "fout")),
        P(("tok", "fout"), "fin"),
    )
    out_specs = (
        P(("tok", "fout"), "fin"),
        P("fin", ("tok", "fout")),
        P("fin", ("tok", "fout")),
        P(("tok", "fout"), "fin"),
    )
    return jax.shard_map(local, mesh=mesh, in_specs=in_specs, out_specs=out_specs, check_vma=False)
```

time: 97.9 us -> 90.7 us (0.926); the launches traced: 96 us -> 90.5 us
  Pallas kernels: 93.7 us -> 88.3 us
    pallas_call x1, Pallas kernels: 91.2 us -> 85.8 us  [local(): pl.pallas_call(kernel, out_shape=(pltpu.VMEM((16, 1024), BF), pltpu.VMEM(...]
where the time goes in v3:
time: 90.7 us; the launch traced here: 90.5 us
  Pallas kernels  88.3 us (97%)
  local copies, waits for them, and re-layouts  1.51 us (2%)
    pallas_call x1, Pallas kernels, local(): pl.pallas_call(kernel, out_shape=(pltpu.VMEM((16, 1024), BF), pltpu.VMEM(...  85.8 us
    pallas_call x1, Pallas kernels, local(): pl.pallas_call(writer, out_shape=(jax.ShapeDtypeStruct((16, 1024), BF), j...  2.48 us

profile of v3, /device:TPU:4, one launch (start us, length us, event | category | flops | bytes accessed | tf_op | source)
XLA Modules:
  0.0 90.5 jit_solution(9416923232303620327)
XLA Ops:
  0.6 0.0 copy-start
  0.6 0.7 copy-done
  1.4 0.0 copy-start.1
  1.4 0.8 copy-done.1
  2.1 85.8 %shard_map.84 = (bf16[16,1024]{1,0:T(8,128)(2,1)S(1)}, bf16[1024,896]{1,0:T(8,128)(2,1)S(1)}, bf16[1024,896]{1,0:T(8,128)(2,1)S(1)}, bf16[896,1024]{1,0:T(8,128)(2,1)S(1)}) custom-call(bf16[16,1024]{1,0:T(8,128)(2,1)S(1)} %copy-done, bf16[16,1024]{1,0:T(8,128)(2,1)S(1)} %copy-done.1, bf16[1024,896]{1,0:T(8,128)(2,1)} %wg_hbm.1, bf16[1024,896]{1,0:T(8,128)(2,1)} %wu_hbm.1, ...), custom_call_target="tpu_custom_call" | custom-call | flops 7516000256 | bytes 11000000 | tf_op jit(solution)/shard_map/pallas_call | solution.py:423
  88.0 2.5 %shard_map.85 = (bf16[16,1024]{1,0:T(8,128)(2,1)}, bf16[1024,896]{1,0:T(8,128)(2,1)}, bf16[1024,896]{1,0:T(8,128)(2,1)}, bf16[896,1024]{1,0:T(8,128)(2,1)}) custom-call(bf16[16,1024]{1,0:T(8,128)(2,1)S(1)} %get-tuple-element.8.refs_0_, bf16[1024,896]{1,0:T(8,128)(2,1)S(1)} %get-tuple-element.9.refs_1_, bf16[1024,896]{1,0:T(8,128)(2,1)S(1)} %get-tuple-element.10.refs_2_, ...), custom_call_target="tpu_custom_call" | custom-call | bytes 11000000 | tf_op jit(solution)/shard_map/pallas_call | solution.py:471
Async XLA Ops:
  0.6 0.8 copy-start
  1.4 0.8 copy-start.1

commit v4 on v3

--- a/solution.py
+++ b/solution.py
@@ -21,7 +21,7 @@
     x_hbm, ct_hbm, wg_hbm, wu_hbm, wd_hbm,
     ig_out, dwg_out, dwu_out, dwd_out,
     xb, xt, ht, wgu, wd, pt, sdn, sup, rdn, rup, gb, igs, igr, ips, ipr, ils, ilr, iys, iyr, igacc,
-    w_sem, g_s, g_r, c0_s, c0_r, cc_s, cc_r,
+    w_sem, g_s, g_r, c_s, c_r, f_s, f_r,
     rs_s, rs_r, ag_s, ag_r, i0_s, i0_r, ix_s, ix_r, il_s, il_r, iy_s, iy_r,
 ):
     tok, z, fout = lax.axis_index("tok"), lax.axis_index("fin"), lax.axis_index("fout")
@@ -94,20 +94,16 @@
         dev = xpeer[k - 1] if r in (0, 3) and k > 0 else ypeer[r]
         return rcopy(xb.at[r, a, blk(k)], xb.at[r, a, blk(k)], g_s.at[r, a, k], g_r.at[r, a, k], dev)
 
-    def c0_copy(a, k, own=True):
+    def c_copy(r, a, k, own=True):
         b = blk(k) if own else (4 - 4 * core) + blk(k) - 4 * core
-        return rcopy(xb.at[0, a, b], xb.at[0, a, b], c0_s.at[a, k], c0_r.at[a, k], partner)
-
-    def cc_copy(r, a, own=True):
-        b = pl.ds(4 * core if own else 4 - 4 * core, 4)
-        return rcopy(xb.at[r, a, b], xb.at[r, a, b], cc_s.at[r, a], cc_r.at[r, a], partner)
+        return rcopy(xb.at[r, a, b], xb.at[r, a, b], c_s.at[r, a, k], c_r.at[r, a, k], partner)
 
     def own_sends():
         for a in (0, 1):
             loads[a].wait()
             for k in (1, 2, 3):
                 start(x_send(0, a, k))
-            start(c0_copy(a, 0))
+            start(c_copy(0, a, 0))
             start(y_send(1, a, 0))
             start(y_send(2, a, 0))
         for a in (0, 1):
@@ -116,7 +112,7 @@
     def row_in(a):
         for k in (1, 2, 3):
             g_recv(0, a, k).wait_recv()
-            start(c0_copy(a, k))
+            start(c_copy(0, a, k))
             start(y_send(1, a, k))
             start(y_send(2, a, k))
 
@@ -127,34 +123,49 @@
 
     nd = [4, 3, 4, 3]
 
-    def hand_over(r):
+    def hand_over(*rounds):
         for a in (0, 1):
             for k in range(4):
-                if r != 3 or k > 0:
-                    g_recv(r, a, k).wait_recv()
-            start(cc_copy(r, a))
+                for r in rounds:
+                    if r != 3 or k > 0:
+                        g_recv(r, a, k).wait_recv()
+                    start(c_copy(r, a, k))
+
+    def first_copy(d, part):
+        b = pl.ds(0, 2) if part == 0 else pl.ds(2, 1)
+        src, dst = (sdn, rdn) if d == 0 else (sup, rup)
+        return rcopy(
+            src.at[0, 0, b], dst.at[0, 0, b], f_s.at[d, part], f_r.at[d, part], zdn if d == 0 else zup
+        )
+
+    def first_sums(part):
+        b = slice(0, 2) if part == 0 else slice(2, 3)
+        sdn[0, 0, b] = pt[0, (z - nd[0] + NZ) % NZ, b].astype(BF)
+        start(first_copy(0, part))
+        sup[0, 0, b] = pt[0, (z + 7 - nd[0]) % NZ, b].astype(BF)
+        start(first_copy(1, part))
 
     def partials(r):
+        for k in range(4):
+            c_copy(r, 0, k, False).wait_recv()
         if r == 0:
-            for k in range(4):
-                c0_copy(0, k, False).wait_recv()
             loads[2].wait()
             loads[3].wait()
-        else:
-            cc_copy(r, 0, False).wait_recv()
         toks = xb[r, 0].reshape(128, 1024)
         both = jnp.dot(toks, wgu[...], preferred_element_type=F32)
         pt[r, :, 0] = both[:, :896].reshape(8, 16, 896)
         pt[r, :, 1] = both[:, 896:].reshape(8, 16, 896)
         if r == 0:
-            for k in range(4):
-                c0_copy(1, k, False).wait_recv()
+            first_sums(0)
             loads[4].wait()
-        else:
-            cc_copy(r, 1, False).wait_recv()
+        for k in range(4):
+            c_copy(r, 1, k, False).wait_recv()
         cots = xb[r, 1].reshape(128, 1024)
         pt[r, :, 2] = lax.dot_general(cots, wd[...], NT, preferred_element_type=F32).reshape(8, 16, 896)
-        send_sums(r, 0)
+        if r == 0:
+            first_sums(1)
+        else:
+            send_sums(r, 0)
         xt[:, r * 128:r * 128 + 128] = toks.T
 
     def dn_copy(r, s):
@@ -162,20 +173,27 @@
 
     def up_copy(r, s):
         return rcopy(sup.at[r, s], rup.at[r, s], rs_s.at[r, 1, s], rs_r.at[r, 1, s], zup)
+
+    def arrived(r, d, s):
+        if r == 0 and s == 0:
+            for part in (0, 1):
+                first_copy(d, part).wait_recv()
+        else:
+            (dn_copy, up_copy)[d](r, s).wait_recv()
 
     def send_sums(r, s):
         n, m = nd[r], 7 - nd[r]
         if s < n:
             mine = pt[r, (z - n + s + NZ + 2 * r) % NZ]
             if s > 0:
-                dn_copy(r, s - 1).wait_recv()
+                arrived(r, 0, s - 1)
                 mine = mine + rdn[r, s - 1].astype(F32)
             sdn[r, s] = mine.astype(BF)
             start(dn_copy(r, s))
         if s < m:
             mine = pt[r, (z + m - s + 2 * r) % NZ]
             if s > 0:
-                up_copy(r, s - 1).wait_recv()
+                arrived(r, 1, s - 1)
                 mine = mine + rup[r, s - 1].astype(F32)
             sup[r, s] = mine.astype(BF)
             start(up_copy(r, s))
@@ -261,16 +279,17 @@
                 if n > 0:
                     px_copy(r, n - 1).start()
 
-    def input_late():
-        part = input_rows([(r, far[r]) for r in range(4)])
-        for r in range(4):
-            ils[r] = part[16 * r:16 * r + 16]
+    def input_late(*rounds):
+        part = input_rows([(r, far[r]) for r in rounds])
+        for n, r in enumerate(rounds):
+            ils[r] = part[16 * n:16 * n + 16]
             if r > 0:
                 start(late_copy(r))
-
-        @pl.when(me != far[0])
-        def _():
-            late_copy(0).start()
+            else:
+
+                @pl.when(me != far[0])
+                def _():
+                    late_copy(0).start()
 
     def row_total(r):
         v = ips[r, x].astype(F32)
@@ -359,20 +378,20 @@
     then(own_sends)
     then(row_in, 0)
     then(row_in, 1)
+    then(partials, 0)
     then(third_in, 0)
     then(third_in, 1)
-    then(partials, 0)
     then(hand_over, 1)
+    then(partials, 1)
     then(hand_over, 2)
-    then(partials, 1)
+    then(stage, 0, 1)
     then(partials, 2)
-    then(stage, 0, 1)
     then(hand_over, 3)
     then(partials, 3)
     then(stage, 1, 1)
+    then(stage, 0, 2)
     then(stage, 2, 1)
-    then(stage, 0, 2)
-    done, last = [2, 1, 1, 0], [2, 0]
+    done, last = [2, 1, 1, 0], [0, 2]
     while min(done) < 6:
         free = [q for q in (3, 2, 1, 0) if q not in last[-2:] and done[q] < 6]
         r = min(free or (3, 2, 1, 0), key=lambda q: done[q])
@@ -390,10 +409,13 @@
     then(stage, 0, 7)
     then(input_early, 0)
     then(pair_early, 1)
-    for r in (3, 2, 1, 0):
-        then(stage, r, 8)
-    then(input_late)
+    then(stage, 3, 8)
+    then(stage, 2, 8)
+    then(input_late, 3, 2)
     then(pair_early, 0)
+    then(stage, 1, 8)
+    then(stage, 0, 8)
+    then(input_late, 1, 0)
     for r in range(4):
         then(turn_hidden, r)
     then(row_sum, 3)
@@ -453,8 +475,8 @@
             vm((16, 1024), F32),
             dma((5,)),
             dma((4, 2, 4)), dma((4, 2, 4)),
-            dma((2, 4)), dma((2, 4)),
-            dma((4, 2)), dma((4, 2)),
+            dma((4, 2, 4)), dma((4, 2, 4)),
+            dma((2, 2)), dma((2, 2)),
             dma((4, 2, 4)), dma((4, 2, 4)),
             dma((4, 2, 4)), dma((4, 2, 4)),
             dma((4, 4)), dma((4, 4)),

time: 90.7 us -> 89.8 us (0.990)
  Pallas kernels: 88.3 us -> 87.3 us
    pallas_call x1, Pallas kernels: 85.8 us -> 84.8 us  [local(): pl.pallas_call(kernel, out_shape=(pltpu.VMEM((16, 1024), BF), pltpu.VMEM(...]
where the time goes in v4:
time: 89.8 us; the launch traced here: 89.6 us
  Pallas kernels  87.3 us (97%)
  local copies, waits for them, and re-layouts  1.51 us (2%)
    pallas_call x1, Pallas kernels, local(): pl.pallas_call(kernel, out_shape=(pltpu.VMEM((16, 1024), BF), pltpu.VMEM(...  84.8 us
    pallas_call x1, Pallas kernels, local(): pl.pallas_call(writer, out_shape=(jax.ShapeDtypeStruct((16, 1024), BF), j...  2.48 us

profile of v4, /device:TPU:4, one launch (start us, length us, event | category | flops | bytes accessed | tf_op | source)
XLA Modules:
  0.0 89.6 jit_solution(859741172584563048)
XLA Ops:
  0.6 0.0 copy-start
  0.6 0.7 copy-done
  1.4 0.0 copy-start.1
  1.4 0.8 copy-done.1
  2.1 84.8 %shard_map.84 = (bf16[16,1024]{1,0:T(8,128)(2,1)S(1)}, bf16[1024,896]{1,0:T(8,128)(2,1)S(1)}, bf16[1024,896]{1,0:T(8,128)(2,1)S(1)}, bf16[896,1024]{1,0:T(8,128)(2,1)S(1)}) custom-call(bf16[16,1024]{1,0:T(8,128)(2,1)S(1)} %copy-done, bf16[16,1024]{1,0:T(8,128)(2,1)S(1)} %copy-done.1, bf16[1024,896]{1,0:T(8,128)(2,1)} %wg_hbm.1, bf16[1024,896]{1,0:T(8,128)(2,1)} %wu_hbm.1, ...), custom_call_target="tpu_custom_call" | custom-call | flops 7516000256 | bytes 11000000 | tf_op jit(solution)/shard_map/pallas_call | solution.py:445
  86.9 2.5 %shard_map.85 = (bf16[16,1024]{1,0:T(8,128)(2,1)}, bf16[1024,896]{1,0:T(8,128)(2,1)}, bf16[1024,896]{1,0:T(8,128)(2,1)}, bf16[896,1024]{1,0:T(8,128)(2,1)}) custom-call(bf16[16,1024]{1,0:T(8,128)(2,1)S(1)} %get-tuple-element.8.refs_0_, bf16[1024,896]{1,0:T(8,128)(2,1)S(1)} %get-tuple-element.9.refs_1_, bf16[1024,896]{1,0:T(8,128)(2,1)S(1)} %get-tuple-element.10.refs_2_, ...), custom_call_target="tpu_custom_call" | custom-call | bytes 11000000 | tf_op jit(solution)/shard_map/pallas_call | solution.py:493
Async XLA Ops:
  0.6 0.8 copy-start
  1.4 0.8 copy-start.1

commit v5 on v4

--- a/solution.py
+++ b/solution.py
@@ -367,6 +367,21 @@
                 igacc[...] = v
 
         ig_out[...] = igacc[...].astype(BF)
+
+    marked = []
+
+    def mark():
+        marked.append(len(sends))
+
+    def drain_marked():
+        for c in sends[:marked[0]]:
+            c.wait_send()
+        del sends[:marked[0]]
+
+    def drain():
+        for c in sends:
+            c.wait_send()
+        sends.clear()
         for r in range(4):
             early_end(r)
 
@@ -388,6 +403,7 @@
     then(partials, 2)
     then(hand_over, 3)
     then(partials, 3)
+    then(mark)
     then(stage, 1, 1)
     then(stage, 0, 2)
     then(stage, 2, 1)
@@ -398,6 +414,7 @@
         done[r] += 1
         last.append(r)
         then(stage, r, done[r])
+    then(drain_marked)
     then(stage, 3, 7)
     then(input_early, 3)
     then(stage, 2, 7)
@@ -423,11 +440,10 @@
     then(row_sum, 1)
     for n in range(3):
         then(weights_part, n)
+    then(drain)
     then(finish)
     for fn, given in steps:
         fn(*given)
-    for c in sends:
-        c.wait_send()
 
 
 def writer(*refs):

time: 89.8 us -> 89.5 us (level)
  no operation moved by 1% of the time
where the time goes in v5:
time: 89.5 us; the launch traced here: 89.3 us
  Pallas kernels  87 us (97%)
  local copies, waits for them, and re-layouts  1.51 us (2%)
    pallas_call x1, Pallas kernels, local(): pl.pallas_call(kernel, out_shape=(pltpu.VMEM((16, 1024), BF), pltpu.VMEM(...  84.5 us
    pallas_call x1, Pallas kernels, local(): pl.pallas_call(writer, out_shape=(jax.ShapeDtypeStruct((16, 1024), BF), j...  2.48 us

profile of v5, /device:TPU:4, one launch (start us, length us, event | category | flops | bytes accessed | tf_op | source)
XLA Modules:
  0.0 89.3 jit_solution(17677761870077583398)
XLA Ops:
  0.6 0.0 copy-start
  0.6 0.7 copy-done
  1.4 0.0 copy-start.1
  1.4 0.8 copy-done.1
  2.1 84.5 %shard_map.84 = (bf16[16,1024]{1,0:T(8,128)(2,1)S(1)}, bf16[1024,896]{1,0:T(8,128)(2,1)S(1)}, bf16[1024,896]{1,0:T(8,128)(2,1)S(1)}, bf16[896,1024]{1,0:T(8,128)(2,1)S(1)}) custom-call(bf16[16,1024]{1,0:T(8,128)(2,1)S(1)} %copy-done, bf16[16,1024]{1,0:T(8,128)(2,1)S(1)} %copy-done.1, bf16[1024,896]{1,0:T(8,128)(2,1)} %wg_hbm.1, bf16[1024,896]{1,0:T(8,128)(2,1)} %wu_hbm.1, ...), custom_call_target="tpu_custom_call" | custom-call | flops 7516000256 | bytes 11000000 | tf_op jit(solution)/shard_map/pallas_call | solution.py:461
  86.7 2.5 %shard_map.85 = (bf16[16,1024]{1,0:T(8,128)(2,1)}, bf16[1024,896]{1,0:T(8,128)(2,1)}, bf16[1024,896]{1,0:T(8,128)(2,1)}, bf16[896,1024]{1,0:T(8,128)(2,1)}) custom-call(bf16[16,1024]{1,0:T(8,128)(2,1)S(1)} %get-tuple-element.8.refs_0_, bf16[1024,896]{1,0:T(8,128)(2,1)S(1)} %get-tuple-element.9.refs_1_, bf16[1024,896]{1,0:T(8,128)(2,1)S(1)} %get-tuple-element.10.refs_2_, ...), custom_call_target="tpu_custom_call" | custom-call | bytes 11000000 | tf_op jit(solution)/shard_map/pallas_call | solution.py:509
Async XLA Ops:
  0.6 0.8 copy-start
  1.4 0.8 copy-start.1
